TPU v7x, 128 devices: a whole 4x4x4 slice. The times are simulated.
128 devices in a mesh: off: 4 (over y), tm: 32 (over x, z, core).
Axes of the slice: x: 4, y: 4, z: 4, core: 2. Of those that a mesh axis runs over, the one named last changes fastest.
Arguments:
- data: bfloat16 [524288, 1024], P('tm', 'off'), may hold values from -6 to 6
- leaf_basis: bfloat16 [4096, 64, 128], P('tm'), may hold values from -0.5 to 0.5
- level_weights: bfloat16 [12, 4096, 64, 128], P(None, 'tm'), may hold values from -0.5 to 0.5
- slowness_table: bfloat16 [1024, 1024], replicated, may hold values from -0.1875 to 0.1875
- model_basis: bfloat16 [4096, 64, 128], P('tm'), may hold values from -0.75 to 0.75
Outputs:
- model: bfloat16 [524288, 1024], P('tm', 'off')
All inputs are finite; a program needn't handle non-finite values.
Results may differ from a plain program's by a relative error of at most 0.03.
Values may be sent and summed in bfloat16 or wider, within the bound.
A program may use at most 192 MiB of HBM per device.

v0:
```python
import jax
import jax.numpy as jnp
from jax import lax
from jax.sharding import PartitionSpec as P


def partner_2(block, axis, distance):
    count = lax.axis_size(axis)
    route = []
    for low in range(count):
        high = low | 1 << distance
        if high != low and high < count:
            route += [(low, high), (high, low)]
    return lax.ppermute(block, axis, route)


def mix_pair(coeffs, partner, level_w):
    stacked = jnp.concatenate([coeffs, partner], axis=1)
    mixed = jnp.einsum("bkr,brn->bkn", level_w, stacked, preferred_element_type=jnp.float32)
    return mixed.astype(jnp.bfloat16)


def local_level(coeffs, level_w, spacing):
    count, rank, cols = coeffs.shape
    grouped = coeffs.reshape(count // (2 * spacing), 2, spacing, rank, cols)
    partner = grouped[:, ::-1].reshape(coeffs.shape)
    return mix_pair(coeffs, partner, level_w)


def local(data, leaf_basis, level_weights, slowness_table, model_basis):
    blocks_dev, rank2, tlen = leaf_basis.shape
    cols_dev = data.shape[1]
    device_bits = lax.axis_size("tm").bit_length() - 1
    local_bits = blocks_dev.bit_length() - 1
    blocks = data.reshape(blocks_dev, tlen, cols_dev)
    coeffs = jnp.einsum(
        "brt,btn->brn", leaf_basis, blocks, preferred_element_type=jnp.float32
    ).astype(jnp.bfloat16)
    for level in range(local_bits):
        coeffs = local_level(coeffs, level_weights[level], 2**level)
    for bit in range(device_bits):
        partner = partner_2(coeffs, "tm", bit)
        coeffs = mix_pair(coeffs, partner, level_weights[local_bits + bit])
    slow_dev = slowness_table.shape[1] // lax.axis_size("off")
    off_index = lax.axis_index("off")
    own_rows = lax.dynamic_slice_in_dim(slowness_table, off_index * cols_dev, cols_dev, 0)
    flat_rows = coeffs.reshape(blocks_dev * rank2, cols_dev)
    summed = lax.psum_scatter(
        lax.dot_general(
            own_rows, flat_rows, (((0,), (1,)), ((), ())), preferred_element_type=jnp.float32
        ).astype(jnp.bfloat16),
        "off",
        scatter_dimension=0,
        tiled=True,
    )
    slow = summed.reshape(slow_dev, blocks_dev, rank2)
    model = jnp.einsum("brt,pbr->btp", model_basis, slow, preferred_element_type=jnp.float32)
    return model.reshape(blocks_dev * tlen, slow_dev).astype(jnp.bfloat16)


def solution(mesh):
    placed = (
        P("tm", "off"),
        P("tm", None, None),
        P(None, "tm", None, None),
        P(),
        P("tm", None, None),
    )
    return jax.shard_map(
        local, mesh=mesh, in_specs=placed, out_specs=P("tm", "off"), check_vma=False
    )
```

profile of v0, /device:TPU:20, one launch (start us, length us, event | category | flops | bytes accessed | tf_op | source)
XLA Modules:
  0.0 674.6 jit_solution(7821864177048068051)
XLA Ops:
  6.5 0.0 copy-start
  6.5 0.0 reduce-scatter.2.cloned.1.call-start
  6.5 7.5 %convolution_convert_fusion.2 = bf16[128,64,256]{2,1,0:T(8,128)(2,1)} fusion(bf16[128,64,128]{2,1,0:T(8,128)(2,1)} %param.6, bf16[128,128,256]{2,1,0:T(8,128)(2,1)} %bitcast.87), kind=kOutput, calls=%fused_computation.55 | convolution fusion | flops 538968064 | bytes 14680064 | tf_op jit(solution)/shard_map/brt,btn->brn/dot_general | solution.py:36
  14.0 4.7 rev.21
  18.7 7.3 %fusion.76 = bf16[128,256,64]{1,2,0:T(8,128)(2,1)} fusion(bf16[128,64,256]{2,1,0:T(8,128)(2,1)} %bitcast.100, bf16[128,64,256]{2,1,0:T(8,128)(2,1)} %convolution_convert_fusion.2, bf16[12,128,64,128]{3,2,1,0:T(8,128)(2,1)} %param.7), kind=kOutput, calls=%fused_computation.62 | convolution fusion | flops 555745280 | bytes 14680064 | tf_op jit(solution)/shard_map/bkr,brn->bkn/dot_general | solution.py:19
  26.0 4.8 rev.22
  30.8 7.3 %fusion.73 = bf16[128,256,64]{1,2,0:T(8,128)(2,1)} fusion(bf16[128,64,256]{2,1,0:T(8,128)(2,1)} %bitcast.101, bf16[128,64,256]{2,1,0:T(8,128)(2,1)} %bitcast.89, bf16[12,128,64,128]{3,2,1,0:T(8,128)(2,1)} %param.7), kind=kOutput, calls=%fused_computation.61 | convolution fusion | flops 555745280 | bytes 14680064 | tf_op jit(solution)/shard_map/bkr,brn->bkn/dot_general | solution.py:19
  38.1 4.8 rev.23
  42.9 7.3 %fusion.70 = bf16[128,256,64]{1,2,0:T(8,128)(2,1)} fusion(bf16[128,64,256]{2,1,0:T(8,128)(2,1)} %bitcast.102, bf16[128,64,256]{2,1,0:T(8,128)(2,1)} %bitcast.91, bf16[12,128,64,128]{3,2,1,0:T(8,128)(2,1)} %param.7), kind=kOutput, calls=%fused_computation.60 | convolution fusion | flops 555745280 | bytes 14680064 | tf_op jit(solution)/shard_map/bkr,brn->bkn/dot_general | solution.py:19
  50.1 4.8 rev.24
  54.9 7.3 %fusion.67 = bf16[128,256,64]{1,2,0:T(8,128)(2,1)} fusion(bf16[128,64,256]{2,1,0:T(8,128)(2,1)} %bitcast.103, bf16[128,64,256]{2,1,0:T(8,128)(2,1)} %bitcast.93, bf16[12,128,64,128]{3,2,1,0:T(8,128)(2,1)} %param.7), kind=kOutput, calls=%fused_computation.59 | convolution fusion | flops 555745280 | bytes 14680064 | tf_op jit(solution)/shard_map/bkr,brn->bkn/dot_general | solution.py:19
  62.2 4.8 rev.25
  67.0 7.3 %fusion.64 = bf16[128,256,64]{1,2,0:T(8,128)(2,1)} fusion(bf16[128,64,256]{2,1,0:T(8,128)(2,1)} %bitcast.104, bf16[128,64,256]{2,1,0:T(8,128)(2,1)} %bitcast.95, bf16[12,128,64,128]{3,2,1,0:T(8,128)(2,1)} %param.7), kind=kOutput, calls=%fused_computation.58 | convolution fusion | flops 555745280 | bytes 14680064 | tf_op jit(solution)/shard_map/bkr,brn->bkn/dot_general | solution.py:19
  74.3 4.8 rev.26
  79.0 7.3 %fusion.61 = bf16[128,256,64]{1,2,0:T(8,128)(2,1)} fusion(bf16[128,64,256]{2,1,0:T(8,128)(2,1)} %bitcast.105, bf16[128,64,256]{2,1,0:T(8,128)(2,1)} %bitcast.97, bf16[12,128,64,128]{3,2,1,0:T(8,128)(2,1)} %param.7), kind=kOutput, calls=%fused_computation.57 | convolution fusion | flops 555745280 | bytes 14680064 | tf_op jit(solution)/shard_map/bkr,brn->bkn/dot_general | solution.py:19
  86.3 4.8 rev.27
  91.1 5.5 convert_bitcast_fusion.4
  96.6 0.1 collective-permute-start
  96.7 7.1 %collective-permute-done = bf16[128,64,256]{2,1,0:T(8,128)(2,1)S(1)} collective-permute-done((bf16[128,64,256]{2,1,0:T(8,128)(2,1)S(1)}, bf16[128,64,256]{2,1,0:T(8,128)(2,1)S(1)}, u32[]{:S(2)}, u32[]{:S(2)}) %collective-permute-start) | collective-permute-done | bytes 4194336 | tf_op jit(solution)/shard_map/ppermute | solution.py:14
  103.8 4.1 convert_bitcast_fusion.3
  108.0 2.0 collective-permute-start.1
  110.0 90.9 %collective-permute-done.1 = bf16[128,64,256]{2,1,0:T(8,128)(2,1)S(1)} collective-permute-done((bf16[128,64,256]{2,1,0:T(8,128)(2,1)S(1)}, bf16[128,64,256]{2,1,0:T(8,128)(2,1)S(1)}, u32[]{:S(2)}, u32[]{:S(2)}) %collective-permute-start.1) | collective-permute-done | bytes 4194336 | tf_op jit(solution)/shard_map/ppermute | solution.py:14
  200.8 4.1 convert_bitcast_fusion.2
  205.0 3.8 collective-permute-start.2
  208.7 90.0 %collective-permute-done.2 = bf16[128,64,256]{2,1,0:T(8,128)(2,1)S(1)} collective-permute-done((bf16[128,64,256]{2,1,0:T(8,128)(2,1)S(1)}, bf16[128,64,256]{2,1,0:T(8,128)(2,1)S(1)}, u32[]{:S(2)}, u32[]{:S(2)}) %collective-permute-start.2) | collective-permute-done | bytes 4194336 | tf_op jit(solution)/shard_map/ppermute | solution.py:14
  298.8 4.1 convert_bitcast_fusion.1
  302.9 1.3 collective-permute-start.3
  304.2 89.9 %collective-permute-done.3 = bf16[128,64,256]{2,1,0:T(8,128)(2,1)S(1)} collective-permute-done((bf16[128,64,256]{2,1,0:T(8,128)(2,1)S(1)}, bf16[128,64,256]{2,1,0:T(8,128)(2,1)S(1)}, u32[]{:S(2)}, u32[]{:S(2)}) %collective-permute-start.3) | collective-permute-done | bytes 4194336 | tf_op jit(solution)/shard_map/ppermute | solution.py:14
  394.1 5.5 convert_bitcast_fusion
  399.7 0.5 collective-permute-start.4
  400.2 91.5 %collective-permute-done.4 = bf16[128,64,256]{2,1,0:T(8,128)(2,1)} collective-permute-done((bf16[128,64,256]{2,1,0:T(8,128)(2,1)}, bf16[128,64,256]{2,1,0:T(8,128)(2,1)}, u32[]{:S(2)}, u32[]{:S(2)}) %collective-permute-start.4) | collective-permute-done | bytes 4194336 | tf_op jit(solution)/shard_map/ppermute | solution.py:14
  491.7 5.3 fusion.48
  497.0 0.0 copy-done
  497.0 8.2 %convolution_convert_fusion = bf16[1024,8192]{1,0:T(8,128)(2,1)} fusion(bf16[8192,256]{1,0:T(8,128)(2,1)S(1)} %bitcast.107, bf16[1024,1024]{1,0:T(8,128)(2,1)S(1)} %copy-done, s32[]{:T(128)S(6)} %select_n.3), kind=kOutput, calls=%fused_computation | convolution fusion | flops 4303355904 | bytes 21495812 | tf_op jit(solution)/shard_map/dot_general | solution.py:49
  505.3 0.0 reduce-scatter.2.cloned.1.call-update
  505.3 147.5 %reduce-scatter.2.cloned.1.call-done = bf16[256,8192]{1,0:T(8,128)(2,1)} async-done(((bf16[1024,8192]{1,0:T(8,128)(2,1)}), bf16[256,8192]{1,0:T(8,128)(2,1)}) %reduce-scatter.2.cloned.1.call-update) | async-done | bytes 4194320 | tf_op jit(solution)/shard_map/reduce_scatter | solution.py:48
  652.7 6.4 copy.7
  659.1 8.6 %convolution_convert_fusion.1 = bf16[128,256,128]{1,2,0:T(8,128)(2,1)} fusion(bf16[256,128,64]{0,2,1:T(8,128)(2,1)} %bitcast.86, bf16[128,64,128]{2,1,0:T(8,128)(2,1)} %param.9), kind=kOutput, calls=%fused_computation.49 | convolution fusion | flops 541065216 | bytes 14680064 | tf_op jit(solution)/shard_map/brt,pbr->btp/dot_general | solution.py:57
Async XLA Ops:
  6.5 490.5 %copy-start = (bf16[1024,1024]{1,0:T(8,128)(2,1)S(1)}, bf16[1024,1024]{1,0:T(8,128)(2,1)}, u32[]{:S(2)}) copy-start(bf16[1024,1024]{1,0:T(8,128)(2,1)} %param.8) | copy-start | bytes 6291460
  6.5 646.2 %reduce-scatter.2.cloned.1.call-start = ((), (), s32[]{:S(2)}) async-start(), calls=%async_computation.1 | async-start | bytes 20971520 | tf_op jit(solution)/shard_map/reduce_scatter | solution.py:48
  96.6 7.2 %collective-permute-start = (bf16[128,64,256]{2,1,0:T(8,128)(2,1)S(1)}, bf16[128,64,256]{2,1,0:T(8,128)(2,1)S(1)}, u32[]{:S(2)}, u32[]{:S(2)}) collective-permute-start(bf16[128,64,256]{2,1,0:T(8,128)(2,1)S(1)} %convert_bitcast_fusion.4), channel_id=1, source_target_pairs={{0,1},{1,0},{2,3},{3,2},{4,5},{5,4},{6,7},{7,6},{8,9},{9,8},{10,11... | collective-permute-start | bytes 12582920 | tf_op jit(solution)/shard_map/ppermute | solution.py:14
  108.0 92.9 %collective-permute-start.1 = (bf16[128,64,256]{2,1,0:T(8,128)(2,1)S(1)}, bf16[128,64,256]{2,1,0:T(8,128)(2,1)S(1)}, u32[]{:S(2)}, u32[]{:S(2)}) collective-permute-start(bf16[128,64,256]{2,1,0:T(8,128)(2,1)S(1)} %convert_bitcast_fusion.3), channel_id=1, source_target_pairs={{0,2},{2,0},{1,3},{3,1},{4,6},{6,4},{5,7},{7,5},{8,10},{10,8},{9,1... | collective-permute-start | bytes 12582920 | tf_op jit(solution)/shard_map/ppermute | solution.py:14
  205.0 93.8 %collective-permute-start.2 = (bf16[128,64,256]{2,1,0:T(8,128)(2,1)S(1)}, bf16[128,64,256]{2,1,0:T(8,128)(2,1)S(1)}, u32[]{:S(2)}, u32[]{:S(2)}) collective-permute-start(bf16[128,64,256]{2,1,0:T(8,128)(2,1)S(1)} %convert_bitcast_fusion.2), channel_id=1, source_target_pairs={{0,4},{4,0},{1,5},{5,1},{2,6},{6,2},{3,7},{7,3},{8,12},{12,8},{9,1... | collective-permute-start | bytes 12582920 | tf_op jit(solution)/shard_map/ppermute | solution.py:14
  302.9 91.2 %collective-permute-start.3 = (bf16[128,64,256]{2,1,0:T(8,128)(2,1)S(1)}, bf16[128,64,256]{2,1,0:T(8,128)(2,1)S(1)}, u32[]{:S(2)}, u32[]{:S(2)}) collective-permute-start(bf16[128,64,256]{2,1,0:T(8,128)(2,1)S(1)} %convert_bitcast_fusion.1), channel_id=1, source_target_pairs={{0,8},{8,0},{1,9},{9,1},{2,10},{10,2},{3,11},{11,3},{4,12},{12,4},... | collective-permute-start | bytes 12582920 | tf_op jit(solution)/shard_map/ppermute | solution.py:14
  399.7 92.1 %collective-permute-start.4 = (bf16[128,64,256]{2,1,0:T(8,128)(2,1)}, bf16[128,64,256]{2,1,0:T(8,128)(2,1)}, u32[]{:S(2)}, u32[]{:S(2)}) collective-permute-start(bf16[128,64,256]{2,1,0:T(8,128)(2,1)} %convert_bitcast_fusion), channel_id=1, source_target_pairs={{0,16},{16,0},{1,17},{17,1},{2,18},{18,2},{3,19},{19,3},{4,20},{20... | collective-permute-start | bytes 12582920 | tf_op jit(solution)/shard_map/ppermute | solution.py:14
Sparse Core Ops, SparseCore 0:
  505.4 147.2 reduce-scatter.1
where the time goes:
time: 678 us; the launch traced here: 675 us
  waiting for transfers between devices  517 us (76%)
  matrix products  96.6 us (14%)
  local copies, waits for them, and re-layouts  39.8 us (6%)
  between operations  13.5 us (2%)
  starting transfers between devices  7.66 us (1%)
    ppermute x5, waiting for transfers between devices, partner_2(): return lax.ppermute(block, axis, route)  370 us
    reduce_scatter x1, waiting for transfers between devices, local(): lax.psum_scatter(lax.dot_general(own_rows, flat_rows, (((0,), (1,)), ((),...  147 us
    dot_general x12, matrix products, mix_pair(): jnp.einsum('bkr,brn->bkn', level_w, stacked, preferred_element_type=jnp.f...  72.3 us
    rev x7, local copies, waits for them, and re-layouts, local_level(): partner = grouped[:, ::-1].reshape(coeffs.shape)  33.5 us
  transfers between devices with their start and end apart: 6, of which 6 were waited for; matrix products, arithmetic and copies ran while one was open for 0% of the time, Pallas kernels for 0%

commit v1 on v0

v1 whole, which is shorter than its diff:
```python
import functools

import jax
import jax.numpy as jnp
from jax import lax
from jax.experimental import pallas as pl
from jax.experimental.pallas import tpu as pltpu
from jax.sharding import PartitionSpec as P

MESH = pl.DeviceIdType.MESH
F32, BF16 = jnp.float32, jnp.bfloat16
CHUNKS = 8
RING = 4
GROUPS = RING * RING
R2, TB, COLS = 64, 128, 256


def place():
    y, tm = lax.axis_index("off"), lax.axis_index("tm")
    return y, tm // 8, (tm // 2) % 4, tm % 2


def device(y, x, z, core):
    return (y, x * 8 + z * 2 + core)


def dot(a, b):
    return jnp.dot(a, b, preferred_element_type=F32)


def pair_weight(own, partner):
    swapped = jnp.concatenate([partner[:, R2:], partner[:, :R2]], axis=1)
    return jnp.concatenate([own, swapped], axis=0)


def mix(weight, low, high):
    out = dot(weight, jnp.concatenate([low, high], axis=0)).astype(BF16)
    return out[:R2], out[R2:]


def signal_all(y, x, z, core):
    barrier = pltpu.get_barrier_semaphore()

    def tell(*there):
        pl.semaphore_signal(barrier, inc=1, device_id=device(*there), device_id_type=MESH)

    tell(y, x, z, 1 - core)
    for d in range(1, GROUPS):
        tell((y + d // RING) % RING, x, (z + d % RING) % RING, core)
    for d in range(1, RING):
        tell(y, (x + d) % RING, z, core)
    for dy in range(RING):
        for d in range(RING):
            source_z = (z + d) % RING
            if dy == 0 and d == 0:
                continue
            pl.when(x != z)(functools.partial(tell, (y + dy) % RING, z, source_z, core))
        for d in range(1, RING):
            there = (x + d) % RING
            new = (x != z) & (there != z)
            if dy > 0:
                new = new | (x == z)
            pl.when(new)(functools.partial(tell, (y + dy) % RING, there, x, core))
    pl.semaphore_wait(barrier, jnp.where(x == z, 28, 42))


def main_kernel(
    data, leaf, weights, table, out,
    data_v, leaf_v, w_v, table_v, c_v, sib_v, e_v, z_v, x_v, s_v, wz_v, wx_v,
    data_sem, leaf_sem, w_sem, table_sem, wz_send, wz_recv, wx_send, wx_recv,
    core_send, core_recv, z_send, z_recv, x_send, x_recv, back_send, back_recv,
):
    y, x, z, core = place()
    per = GROUPS // CHUNKS

    def load_data(p):
        return pltpu.make_async_copy(data.at[pl.ds(p * per, per)], data_v.at[pl.ds(p * per, per)], data_sem.at[p])

    def load_leaf(p):
        return pltpu.make_async_copy(leaf.at[pl.ds(p * per, per)], leaf_v.at[pl.ds(p * per, per)], leaf_sem.at[p])

    def load_w(level):
        return pltpu.make_async_copy(weights.at[level], w_v.at[level], w_sem.at[level])

    load_table = pltpu.make_async_copy(table, table_v, table_sem)
    for p in range(CHUNKS):
        load_leaf(p).start()
        load_data(p).start()
    for level in range(8):
        load_w(level).start()
    load_table.start()

    signal_all(y, x, z, core)

    def remote(src, dst, send, recv, there):
        return pltpu.make_async_remote_copy(
            src_ref=src, dst_ref=dst, send_sem=send, recv_sem=recv, device_id=device(*there), device_id_type=MESH
        )

    for d in range(1, RING):
        to = (z + d) % RING
        remote(weights.at[pl.ds(8, 2), RING * y + to], wz_v.at[z], wz_send, wz_recv, (y, x, to, core)).start()
    pltpu.make_async_copy(weights.at[pl.ds(8, 2), RING * y + z], wz_v.at[z], wz_recv).start()
    for d in range(RING):
        to = (z + d) % RING
        src = weights.at[pl.ds(10, 2), RING * y + to]

        def send_wx(src=src, to=to):
            remote(src, wx_v.at[x], wx_send, wx_recv, (y, z, to, core)).start()

        if d == 0:
            pl.when(x != z)(send_wx)

            @pl.when(x == z)
            def _():
                pltpu.make_async_copy(src, wx_v.at[x], wx_recv).start()
        else:
            send_wx()

    def leaf_part(p, carry):
        load_leaf(p).wait()
        load_data(p).wait()

        def some(j, carry):
            for u in range(4):
                n = j * 4 + u
                a, k = p * per + n // CHUNKS, n % CHUNKS
                c_v[a, k] = dot(leaf_v[a, k], data_v[a, k]).astype(BF16)
            return carry

        return lax.fori_loop(0, per * CHUNKS // 4, some, carry)

    lax.fori_loop(0, CHUNKS, leaf_part, 0)

    def mix_blocks(level, low, high):
        weight = pair_weight(w_v[(level, *low)], w_v[(level, *high)])
        c_v[low], c_v[high] = mix(weight, c_v[low], c_v[high])

    for level in range(6):
        load_w(level).wait()
        spacing = 2**level

        def some(j, carry, level=level, spacing=spacing):
            for u in range(4):
                n = j * 4 + u
                low = (n // spacing) * (2 * spacing) + n % spacing
                high = low + spacing
                mix_blocks(level, (low // CHUNKS, low % CHUNKS), (high // CHUNKS, high % CHUNKS))
            return carry

        lax.fori_loop(0, 16, some, 0)
    load_w(6).wait()
    load_w(7).wait()

    def send_core(k):
        return remote(c_v.at[:, k], sib_v.at[:, k], core_send.at[k], core_recv.at[k], (y, x, z, 1 - core))

    def level_6(k):
        def some(j, carry):
            for u in range(4):
                a = j * 4 + u
                mix_blocks(6, (a, k), (a + GROUPS // 2, k))
            return carry

        lax.fori_loop(0, GROUPS // 8, some, 0)
        send_core(k).start()

    def level_7(k):
        send_core(k).wait_recv()

        def some(j, carry):
            for u in range(4):
                a = j * 4 + u
                stacked = jnp.concatenate([c_v[a, k], sib_v[a, k]], axis=0)
                e_v[a, k] = dot(w_v[7, a, k], stacked).astype(BF16)
            return carry

        lax.fori_loop(0, GROUPS // 4, some, 0)
        for d in (5, 7, 13, 15, 1, 3, 4, 12, 6, 9, 11, 14, 2, 8, 10):
            ty, tz = (y + d // RING) % RING, (z + d % RING) % RING
            remote(e_v.at[RING * ty + tz, k], z_v.at[k, y, z], z_send.at[k], z_recv.at[k], (ty, x, tz, core)).start()
        pltpu.make_async_copy(e_v.at[RING * y + z, k], z_v.at[k, y, z], z_recv.at[k]).start()

    def two_levels(k, w, get, put):
        first = [pair_weight(w[b, 0, k], w[b + 1, 0, k]) for b in (0, 2)]
        second = [pair_weight(w[b, 1, k], w[b + 2, 1, k]) for b in (0, 1)]
        for q in range(RING):
            b0, b1 = mix(first[0], get(0, q), get(1, q))
            b2, b3 = mix(first[1], get(2, q), get(3, q))
            b0, b2 = mix(second[0], b0, b2)
            b1, b3 = mix(second[1], b1, b3)
            for b, value in enumerate((b0, b1, b2, b3)):
                put(b, q, value)

    def levels_z(k):
        pltpu.make_async_copy(z_v.at[k], z_v.at[k], z_recv.at[k]).wait()

        def put(b, q, value):
            z_v[k, q, b] = value

        two_levels(k, wz_v, lambda b, q: z_v[k, q, b], put)
        for d in (1, 3, 2):
            to = (x + d) % RING
            remote(z_v.at[k, :, to], x_v.at[k, x], x_send.at[k], x_recv.at[k], (y, to, z, core)).start()
        pltpu.make_async_copy(z_v.at[k, :, x], x_v.at[k, x], x_recv.at[k]).start()

    def levels_x(k):
        pltpu.make_async_copy(x_v.at[k], x_v.at[k], x_recv.at[k]).wait()

        def put(b, q, value):
            x_v[k, b, q] = value

        two_levels(k, wx_v, lambda b, q: x_v[k, b, q], put)
        for part in range(RING):
            total = jnp.zeros((RING * R2, COLS), F32)
            for q in range(RING):
                rows = x_v[k, :, q].reshape(RING * R2, COLS)
                total += dot(rows, table_v[pl.ds(q * COLS, COLS), pl.ds(part * COLS, COLS)])
            s_v[k, :, part] = total.astype(BF16).reshape(RING, R2, COLS)
        mine = RING * y + z
        for d in (5, 7, 13, 15, 1, 3, 4, 12, 6, 9, 11, 14, 2, 8, 10, 0):
            ty, tx = (y + d // RING) % RING, (x + d % RING) % RING

            def send_back(ty=ty, tx=tx):
                remote(s_v.at[k, tx, ty], out.at[mine, k], back_send.at[k], back_recv.at[k], (ty, tx, x, core)).start()

            if d == 0:
                pl.when(x != z)(send_back)

                @pl.when(x == z)
                def _():
                    pltpu.make_async_copy(s_v.at[k, x, y], out.at[mine, k], back_recv.at[k]).start()
            else:
                send_back()

    def step(t, carry):
        pl.when(t < CHUNKS)(lambda: level_6(t))
        pl.when((t >= 1) & (t < CHUNKS + 1))(lambda: level_7(t - 1))

        @pl.when(t == 2)
        def _():
            pltpu.make_async_copy(wz_v, wz_v, wz_recv).wait()

        pl.when((t >= 2) & (t < CHUNKS + 2))(lambda: levels_z(t - 2))

        @pl.when(t == 3)
        def _():
            pltpu.make_async_copy(wx_v, wx_v, wx_recv).wait()
            load_table.wait()

        pl.when(t >= 3)(lambda: levels_x(t - 3))
        return carry

    lax.fori_loop(0, CHUNKS + 3, step, 0)

    def finish(k, carry):
        send_core(k).wait_send()
        pltpu.make_async_copy(e_v.at[pl.ds(0, 15), k], e_v.at[pl.ds(0, 15), k], z_send.at[k]).wait()
        pltpu.make_async_copy(x_v.at[k, pl.ds(0, 3)], x_v.at[k, pl.ds(0, 3)], x_send.at[k]).wait()

        @pl.when(x != z)
        def _():
            pltpu.make_async_copy(s_v.at[k], s_v.at[k], back_send.at[k]).wait()

        @pl.when(x == z)
        def _():
            pltpu.make_async_copy(e_v.at[pl.ds(0, 15), k], e_v.at[pl.ds(0, 15), k], back_send.at[k]).wait()

        pltpu.make_async_copy(out.at[:, k], out.at[:, k], back_recv.at[k]).wait()
        return carry

    lax.fori_loop(0, CHUNKS, finish, 0)
    pltpu.make_async_copy(wz_v.at[pl.ds(0, 3)], wz_v.at[pl.ds(0, 3)], wz_send).wait()

    @pl.when(x != z)
    def _():
        pltpu.make_async_copy(wx_v, wx_v, wx_send).wait()

    @pl.when(x == z)
    def _():
        pltpu.make_async_copy(wx_v.at[pl.ds(0, 3)], wx_v.at[pl.ds(0, 3)], wx_send).wait()


def model_kernel(basis, slow, out):
    def some(j, carry):
        for u in range(4):
            n = j * 4 + u
            rows = lax.dot_general(basis[n], slow[n], (((0,), (0,)), ((), ())), preferred_element_type=F32)
            out[n] = rows.astype(BF16)
        return carry

    lax.fori_loop(0, basis.shape[0] // 4, some, 0)


def local(data, leaf_basis, level_weights, slowness_table, model_basis):
    any_space = pl.BlockSpec(memory_space=pl.ANY)
    levels = level_weights.shape[0]
    dma, vmem = pltpu.SemaphoreType.DMA, pltpu.VMEM
    slow = pl.pallas_call(
        main_kernel,
        out_shape=jax.ShapeDtypeStruct((GROUPS, CHUNKS, R2, COLS), BF16),
        in_specs=[any_space] * 4,
        out_specs=any_space,
        scratch_shapes=[
            vmem((GROUPS, CHUNKS, TB, COLS), BF16),
            vmem((GROUPS, CHUNKS, R2, TB), BF16),
            vmem((8, GROUPS, CHUNKS, R2, TB), BF16),
            vmem(slowness_table.shape, BF16),
            vmem((GROUPS, CHUNKS, R2, COLS), BF16),
            vmem((GROUPS, CHUNKS, R2, COLS), BF16),
            vmem((GROUPS, CHUNKS, R2, COLS), BF16),
            vmem((CHUNKS, RING, RING, R2, COLS), BF16),
            vmem((CHUNKS, RING, RING, R2, COLS), BF16),
            vmem((CHUNKS, RING, RING, R2, COLS), BF16),
            vmem((RING, 2, CHUNKS, R2, TB), BF16),
            vmem((RING, 2, CHUNKS, R2, TB), BF16),
            dma((CHUNKS,)), dma((CHUNKS,)), dma((8,)), dma,
            dma, dma, dma, dma,
            dma((CHUNKS,)), dma((CHUNKS,)), dma((CHUNKS,)), dma((CHUNKS,)),
            dma((CHUNKS,)), dma((CHUNKS,)), dma((CHUNKS,)), dma((CHUNKS,)),
        ],
        compiler_params=pltpu.CompilerParams(collective_id=0, has_side_effects=True, vmem_limit_bytes=58 << 20),
    )(
        data.reshape(GROUPS, CHUNKS, TB, COLS),
        leaf_basis.reshape(GROUPS, CHUNKS, R2, TB),
        level_weights.reshape(levels, GROUPS, CHUNKS, R2, TB),
        slowness_table,
    )
    blocks = GROUPS * CHUNKS
    step = 16
    model = pl.pallas_call(
        model_kernel,
        grid=(blocks // step,),
        out_shape=jax.ShapeDtypeStruct((blocks, TB, COLS), BF16),
        in_specs=[
            pl.BlockSpec((step, R2, TB), lambda n: (n, 0, 0)),
            pl.BlockSpec((step, R2, COLS), lambda n: (n, 0, 0)),
        ],
        out_specs=pl.BlockSpec((step, TB, COLS), lambda n: (n, 0, 0)),
        compiler_params=pltpu.CompilerParams(vmem_limit_bytes=24 << 20),
    )(model_basis, slow.reshape(blocks, R2, COLS))
    return model.reshape(blocks * TB, COLS)


def solution(mesh):
    placed = (
        P("tm", "off"),
        P("tm", None, None),
        P(None, "tm", None, None),
        P(),
        P("tm", None, None),
    )
    return jax.shard_map(local, mesh=mesh, in_specs=placed, out_specs=P("tm", "off"), check_vma=False)
```

time: 678 us -> 216 us (0.32)
  waiting for transfers between devices: 517 us -> 0 us
  Pallas kernels: 0 us -> 212 us
  matrix products: 96.6 us -> 0 us
  local copies, waits for them, and re-layouts: 39.8 us -> 2.18 us
  between operations: 13.5 us -> 0.03 us
  starting transfers between devices: 7.66 us -> 0 us
    ppermute x5 -> x0, waiting for transfers between devices: 370 us -> none  [partner_2(): return lax.ppermute(block, axis, route)]
    pallas_call x0 -> x2, Pallas kernels: none -> 212 us  [the longest x1 202 us: local(): pl.pallas_call(main_kernel, out_shape=jax.ShapeDtypeStruct((GROUPS, CHUNK...]
    reduce_scatter x1 -> x0, waiting for transfers between devices: 147 us -> none  [local(): lax.psum_scatter(lax.dot_general(own_rows, flat_rows, (((0,), (1,)), ((),...]
    dot_general x15 -> x0, matrix products: 96.6 us -> none  [the longest x12 72.3 us: mix_pair(): jnp.einsum('bkr,brn->bkn', level_w, stacked, preferred_element_type=jnp.f...]
    rev x7 -> x0, local copies, waits for them, and re-layouts: 33.5 us -> none  [local_level(): partner = grouped[:, ::-1].reshape(coeffs.shape)]
    ppermute x5 -> x0, starting transfers between devices: 7.66 us -> none  [partner_2(): return lax.ppermute(block, axis, route)]
  transfers between devices with their start and end apart: 6 -> 0, of which waited for: 6 -> 0; matrix products, arithmetic and copies ran while one was open for 0% -> 0% of each run, Pallas kernels for 0% -> 0%
where the time goes in v1:
time: 216 us; the launch traced here: 214 us
  Pallas kernels  212 us (98%)
  local copies, waits for them, and re-layouts  2.18 us (1%)
    pallas_call x1, Pallas kernels, local(): pl.pallas_call(main_kernel, out_shape=jax.ShapeDtypeStruct((GROUPS, CHUNK...  202 us
    pallas_call x1, Pallas kernels, local(): pl.pallas_call(model_kernel, grid=(blocks // step,), out_shape=jax.ShapeD...  9.17 us

profile of v1, /device:TPU:20, one launch (start us, length us, event | category | flops | bytes accessed | tf_op | source)
XLA Modules:
  0.0 213.8 jit_solution(13937011467450417127)
XLA Ops:
  0.0 0.0 copy-start.1
  0.0 202.4 %shard_map.55 = bf16[16,8,64,256]{3,2,1,0:T(8,128)(2,1)} custom-call(bf16[16,8,128,256]{3,2,1,0:T(8,128)(2,1)} %bitcast.7, bf16[16,8,64,128]{3,2,1,0:T(8,128)(2,1)} %bitcast.8, bf16[12,16,8,64,128]{4,3,2,1,0:T(8,128)(2,1)} %bitcast.6, bf16[1024,1024]{1,0:T(8,128)(2,1)} %table.1), custom_call_target="tpu_custom_call" | custom-call | tf_op jit(solution)/shard_map/pallas_call | solution.py:299
  202.4 0.0 copy-done.1
  202.4 0.0 copy-start
  202.4 2.2 %copy-done = bf16[16,8,64,256]{3,2,1,0:T(8,128)(2,1)S(1)} copy-done((bf16[16,8,64,256]{3,2,1,0:T(8,128)(2,1)S(1)}, bf16[16,8,64,256]{3,2,1,0:T(8,128)(2,1)}, u32[]{:S(2)}) %copy-start) | copy-done | bytes 4194328
  204.6 9.2 %shard_map.56 = bf16[128,128,256]{2,1,0:T(8,128)(2,1)} custom-call(bf16[128,64,128]{2,1,0:T(8,128)(2,1)S(1)} %copy-done.1, bf16[128,64,256]{2,1,0:T(8,128)(2,1)S(1)} %bitcast.5), custom_call_target="tpu_custom_call" | custom-call | tf_op jit(solution)/shard_map/pallas_call | solution.py:331
Async XLA Ops:
  0.0 202.4 %copy-start.1 = (bf16[128,64,128]{2,1,0:T(8,128)(2,1)S(1)}, bf16[128,64,128]{2,1,0:T(8,128)(2,1)}, u32[]{:S(2)}) copy-start(bf16[128,64,128]{2,1,0:T(8,128)(2,1)} %basis.1) | copy-start | bytes 6291460
  202.4 2.2 %copy-start = (bf16[16,8,64,256]{3,2,1,0:T(8,128)(2,1)S(1)}, bf16[16,8,64,256]{3,2,1,0:T(8,128)(2,1)}, u32[]{:S(2)}) copy-start(bf16[16,8,64,256]{3,2,1,0:T(8,128)(2,1)} %shard_map.55) | copy-start | bytes 12582916

commit v2 on v1

--- a/solution.py
+++ b/solution.py
@@ -12,6 +12,7 @@
 CHUNKS = 8
 RING = 4
 GROUPS = RING * RING
+BATCH = 8
 R2, TB, COLS = 64, 128, 256
 
 
@@ -66,8 +67,8 @@
 
 def main_kernel(
     data, leaf, weights, table, out,
-    data_v, leaf_v, w_v, table_v, c_v, sib_v, e_v, z_v, x_v, s_v, wz_v, wx_v,
-    data_sem, leaf_sem, w_sem, table_sem, wz_send, wz_recv, wx_send, wx_recv,
+    data_v, leaf_v, w_v, table_v, c_v, sib_v, e_v, z_v, x_v, s_v, wy_v, wz_v, wx_v,
+    data_sem, leaf_sem, w_sem, table_sem, wy_send, wy_recv, wz_send, wz_recv, wx_send, wx_recv,
     core_send, core_recv, z_send, z_recv, x_send, x_recv, back_send, back_recv,
 ):
     y, x, z, core = place()
@@ -97,85 +98,75 @@
             src_ref=src, dst_ref=dst, send_sem=send, recv_sem=recv, device_id=device(*there), device_id_type=MESH
         )
 
-    for d in range(1, RING):
-        to = (z + d) % RING
-        remote(weights.at[pl.ds(8, 2), RING * y + to], wz_v.at[z], wz_send, wz_recv, (y, x, to, core)).start()
-    pltpu.make_async_copy(weights.at[pl.ds(8, 2), RING * y + z], wz_v.at[z], wz_recv).start()
-    for d in range(RING):
-        to = (z + d) % RING
-        src = weights.at[pl.ds(10, 2), RING * y + to]
-
-        def send_wx(src=src, to=to):
-            remote(src, wx_v.at[x], wx_send, wx_recv, (y, z, to, core)).start()
-
-        if d == 0:
-            pl.when(x != z)(send_wx)
-
-            @pl.when(x == z)
-            def _():
-                pltpu.make_async_copy(src, wx_v.at[x], wx_recv).start()
-        else:
-            send_wx()
+    for first, dst, send, recv in ((10, wy_v, wy_send, wy_recv), (8, wz_v, wz_send, wz_recv)):
+        for d in (1, 3, 2):
+            to = (z + d) % RING
+            remote(weights.at[pl.ds(first, 2), RING * y + to], dst.at[z], send, recv, (y, x, to, core)).start()
+        pltpu.make_async_copy(weights.at[pl.ds(first, 2), RING * y + z], dst.at[z], recv).start()
+
+    def forward_weights():
+        pltpu.make_async_copy(wy_v, wy_v, wy_recv).wait()
+        for d in (1, 3, 2):
+            to = (x + d) % RING
+            remote(wy_v.at[to], wx_v.at[x], wx_send, wx_recv, (y, to, z, core)).start()
+        pltpu.make_async_copy(wy_v.at[x], wx_v.at[x], wx_recv).start()
 
     def leaf_part(p, carry):
         load_leaf(p).wait()
         load_data(p).wait()
 
         def some(j, carry):
-            for u in range(4):
-                n = j * 4 + u
-                a, k = p * per + n // CHUNKS, n % CHUNKS
-                c_v[a, k] = dot(leaf_v[a, k], data_v[a, k]).astype(BF16)
+            a = p * per + j
+            parts = [dot(leaf_v[a, k], data_v[a, k]).astype(BF16) for k in range(CHUNKS)]
+            for k in range(CHUNKS):
+                c_v[a, k] = parts[k]
             return carry
 
-        return lax.fori_loop(0, per * CHUNKS // 4, some, carry)
+        return lax.fori_loop(0, per, some, carry)
 
     lax.fori_loop(0, CHUNKS, leaf_part, 0)
 
-    def mix_blocks(level, low, high):
-        weight = pair_weight(w_v[(level, *low)], w_v[(level, *high)])
-        c_v[low], c_v[high] = mix(weight, c_v[low], c_v[high])
+    def mix_blocks(level, pairs):
+        mixed = [
+            mix(pair_weight(w_v[(level, *low)], w_v[(level, *high)]), c_v[low], c_v[high]) for low, high in pairs
+        ]
+        for (low, high), (first, second) in zip(pairs, mixed):
+            c_v[low], c_v[high] = first, second
 
     for level in range(6):
         load_w(level).wait()
         spacing = 2**level
 
         def some(j, carry, level=level, spacing=spacing):
-            for u in range(4):
-                n = j * 4 + u
+            pairs = []
+            for u in range(BATCH):
+                n = j * BATCH + u
                 low = (n // spacing) * (2 * spacing) + n % spacing
                 high = low + spacing
-                mix_blocks(level, (low // CHUNKS, low % CHUNKS), (high // CHUNKS, high % CHUNKS))
+                pairs.append(((low // CHUNKS, low % CHUNKS), (high // CHUNKS, high % CHUNKS)))
+            mix_blocks(level, pairs)
             return carry
 
-        lax.fori_loop(0, 16, some, 0)
+        lax.fori_loop(0, GROUPS * CHUNKS // 2 // BATCH, some, 0)
     load_w(6).wait()
     load_w(7).wait()
+    forward_weights()
 
     def send_core(k):
         return remote(c_v.at[:, k], sib_v.at[:, k], core_send.at[k], core_recv.at[k], (y, x, z, 1 - core))
 
     def level_6(k):
-        def some(j, carry):
-            for u in range(4):
-                a = j * 4 + u
-                mix_blocks(6, (a, k), (a + GROUPS // 2, k))
-            return carry
-
-        lax.fori_loop(0, GROUPS // 8, some, 0)
+        mix_blocks(6, [((a, k), (a + GROUPS // 2, k)) for a in range(GROUPS // 2)])
         send_core(k).start()
 
     def level_7(k):
         send_core(k).wait_recv()
 
-        def some(j, carry):
-            for u in range(4):
-                a = j * 4 + u
-                stacked = jnp.concatenate([c_v[a, k], sib_v[a, k]], axis=0)
-                e_v[a, k] = dot(w_v[7, a, k], stacked).astype(BF16)
-            return carry
-
-        lax.fori_loop(0, GROUPS // 4, some, 0)
+        mixed = [
+            dot(w_v[7, a, k], jnp.concatenate([c_v[a, k], sib_v[a, k]], axis=0)).astype(BF16) for a in range(GROUPS)
+        ]
+        for a in range(GROUPS):
+            e_v[a, k] = mixed[a]
         for d in (5, 7, 13, 15, 1, 3, 4, 12, 6, 9, 11, 14, 2, 8, 10):
             ty, tz = (y + d // RING) % RING, (z + d % RING) % RING
             remote(e_v.at[RING * ty + tz, k], z_v.at[k, y, z], z_send.at[k], z_recv.at[k], (ty, x, tz, core)).start()
@@ -184,13 +175,18 @@
     def two_levels(k, w, get, put):
         first = [pair_weight(w[b, 0, k], w[b + 1, 0, k]) for b in (0, 2)]
         second = [pair_weight(w[b, 1, k], w[b + 2, 1, k]) for b in (0, 1)]
+        results = []
         for q in range(RING):
             b0, b1 = mix(first[0], get(0, q), get(1, q))
             b2, b3 = mix(first[1], get(2, q), get(3, q))
+            results.append((b0, b1, b2, b3))
+        for q, (b0, b1, b2, b3) in enumerate(results):
             b0, b2 = mix(second[0], b0, b2)
             b1, b3 = mix(second[1], b1, b3)
-            for b, value in enumerate((b0, b1, b2, b3)):
-                put(b, q, value)
+            results[q] = (b0, b1, b2, b3)
+        for q in range(RING):
+            for b in range(RING):
+                put(b, q, results[q][b])
 
     def levels_z(k):
         pltpu.make_async_copy(z_v.at[k], z_v.at[k], z_recv.at[k]).wait()
@@ -212,10 +208,8 @@
 
         two_levels(k, wx_v, lambda b, q: x_v[k, b, q], put)
         for part in range(RING):
-            total = jnp.zeros((RING * R2, COLS), F32)
-            for q in range(RING):
-                rows = x_v[k, :, q].reshape(RING * R2, COLS)
-                total += dot(rows, table_v[pl.ds(q * COLS, COLS), pl.ds(part * COLS, COLS)])
+            rows = jnp.concatenate([x_v[k, :, q].reshape(RING * R2, COLS) for q in range(RING)], axis=1)
+            total = dot(rows, table_v[:, pl.ds(part * COLS, COLS)])
             s_v[k, :, part] = total.astype(BF16).reshape(RING, R2, COLS)
         mine = RING * y + z
         for d in (5, 7, 13, 15, 1, 3, 4, 12, 6, 9, 11, 14, 2, 8, 10, 0):
@@ -270,26 +264,21 @@
         return carry
 
     lax.fori_loop(0, CHUNKS, finish, 0)
-    pltpu.make_async_copy(wz_v.at[pl.ds(0, 3)], wz_v.at[pl.ds(0, 3)], wz_send).wait()
-
-    @pl.when(x != z)
-    def _():
-        pltpu.make_async_copy(wx_v, wx_v, wx_send).wait()
-
-    @pl.when(x == z)
-    def _():
-        pltpu.make_async_copy(wx_v.at[pl.ds(0, 3)], wx_v.at[pl.ds(0, 3)], wx_send).wait()
+    for held, sem in ((wy_v, wy_send), (wz_v, wz_send), (wx_v, wx_send)):
+        pltpu.make_async_copy(held.at[pl.ds(0, 3)], held.at[pl.ds(0, 3)], sem).wait()
 
 
 def model_kernel(basis, slow, out):
     def some(j, carry):
-        for u in range(4):
-            n = j * 4 + u
-            rows = lax.dot_general(basis[n], slow[n], (((0,), (0,)), ((), ())), preferred_element_type=F32)
-            out[n] = rows.astype(BF16)
+        rows = [
+            lax.dot_general(basis[n], slow[n], (((0,), (0,)), ((), ())), preferred_element_type=F32).astype(BF16)
+            for n in [j * BATCH + u for u in range(BATCH)]
+        ]
+        for u in range(BATCH):
+            out[j * BATCH + u] = rows[u]
         return carry
 
-    lax.fori_loop(0, basis.shape[0] // 4, some, 0)
+    lax.fori_loop(0, basis.shape[0] // BATCH, some, 0)
 
 
 def local(data, leaf_basis, level_weights, slowness_table, model_basis):
@@ -314,8 +303,9 @@
             vmem((CHUNKS, RING, RING, R2, COLS), BF16),
             vmem((RING, 2, CHUNKS, R2, TB), BF16),
             vmem((RING, 2, CHUNKS, R2, TB), BF16),
+            vmem((RING, 2, CHUNKS, R2, TB), BF16),
             dma((CHUNKS,)), dma((CHUNKS,)), dma((8,)), dma,
-            dma, dma, dma, dma,
+            dma, dma, dma, dma, dma, dma,
             dma((CHUNKS,)), dma((CHUNKS,)), dma((CHUNKS,)), dma((CHUNKS,)),
             dma((CHUNKS,)), dma((CHUNKS,)), dma((CHUNKS,)), dma((CHUNKS,)),
         ],
@@ -337,7 +327,7 @@
             pl.BlockSpec((step, R2, COLS), lambda n: (n, 0, 0)),
         ],
         out_specs=pl.BlockSpec((step, TB, COLS), lambda n: (n, 0, 0)),
-        compiler_params=pltpu.CompilerParams(vmem_limit_bytes=24 << 20),
+        compiler_params=pltpu.CompilerParams(vmem_limit_bytes=58 << 20),
     )(model_basis, slow.reshape(blocks, R2, COLS))
     return model.reshape(blocks * TB, COLS)
 

time: 216 us -> 162 us (0.75)
  Pallas kernels: 212 us -> 162 us
  local copies, waits for them, and re-layouts: 2.18 us -> 0 us
    pallas_call x1, Pallas kernels: 202 us -> 152 us  [local(): pl.pallas_call(main_kernel, out_shape=jax.ShapeDtypeStruct((GROUPS, CHUNK...]
    unnamed x4 -> x0, local copies, waits for them, and re-layouts: 2.18 us -> none
where the time goes in v2:
time: 162 us
  Pallas kernels  162 us (100%)
    pallas_call x1, Pallas kernels, local(): pl.pallas_call(main_kernel, out_shape=jax.ShapeDtypeStruct((GROUPS, CHUNK...  152 us
    pallas_call x1, Pallas kernels, local(): pl.pallas_call(model_kernel, grid=(blocks // step,), out_shape=jax.ShapeD...  10.1 us

profile of v2, /device:TPU:20, one launch (start us, length us, event | category | flops | bytes accessed | tf_op | source)
XLA Modules:
  0.0 161.8 jit_solution(16937542475714784980)
XLA Ops:
  0.0 151.7 %shard_map.55 = bf16[16,8,64,256]{3,2,1,0:T(8,128)(2,1)} custom-call(bf16[16,8,128,256]{3,2,1,0:T(8,128)(2,1)} %bitcast.7, bf16[16,8,64,128]{3,2,1,0:T(8,128)(2,1)} %bitcast.8, bf16[12,16,8,64,128]{4,3,2,1,0:T(8,128)(2,1)} %bitcast.5, bf16[1024,1024]{1,0:T(8,128)(2,1)} %table.1), custom_call_target="tpu_custom_call" | custom-call | tf_op jit(solution)/shard_map/pallas_call | solution.py:288
  151.7 10.1 %shard_map.56 = bf16[128,128,256]{2,1,0:T(8,128)(2,1)} custom-call(bf16[128,64,128]{2,1,0:T(8,128)(2,1)} %basis.1, bf16[128,64,256]{2,1,0:T(8,128)(2,1)} %bitcast.6), custom_call_target="tpu_custom_call" | custom-call | tf_op jit(solution)/shard_map/pallas_call | solution.py:321

commit v3 on v2

--- a/solution.py
+++ b/solution.py
@@ -12,8 +12,9 @@
 CHUNKS = 8
 RING = 4
 GROUPS = RING * RING
-BATCH = 8
+BATCH = 16
 R2, TB, COLS = 64, 128, 256
+HALF = COLS // 2
 
 
 def place():
@@ -39,7 +40,7 @@
     return out[:R2], out[R2:]
 
 
-def signal_all(y, x, z, core):
+def tell_all(y, x, z, core):
     barrier = pltpu.get_barrier_semaphore()
 
     def tell(*there):
@@ -62,7 +63,6 @@
             if dy > 0:
                 new = new | (x == z)
             pl.when(new)(functools.partial(tell, (y + dy) % RING, there, x, core))
-    pl.semaphore_wait(barrier, jnp.where(x == z, 28, 42))
 
 
 def main_kernel(
@@ -83,26 +83,45 @@
     def load_w(level):
         return pltpu.make_async_copy(weights.at[level], w_v.at[level], w_sem.at[level])
 
-    load_table = pltpu.make_async_copy(table, table_v, table_sem)
     for p in range(CHUNKS):
         load_leaf(p).start()
         load_data(p).start()
     for level in range(8):
         load_w(level).start()
-    load_table.start()
-
-    signal_all(y, x, z, core)
+    for half in range(2):
+        for q in range(RING):
+            rows = table.at[pl.ds(q * COLS + half * HALF, HALF)]
+            pltpu.make_async_copy(rows, table_v.at[pl.ds((half * RING + q) * HALF, HALF)], table_sem).start()
+
+    tell_all(y, x, z, core)
 
     def remote(src, dst, send, recv, there):
         return pltpu.make_async_remote_copy(
             src_ref=src, dst_ref=dst, send_sem=send, recv_sem=recv, device_id=device(*there), device_id_type=MESH
         )
+
+    def leaf_part(p, carry):
+        load_leaf(p).wait()
+        load_data(p).wait()
+
+        def some(j, carry):
+            a = p * per + j
+            parts = [dot(leaf_v[a, k], data_v[a, k]).astype(BF16) for k in range(CHUNKS)]
+            for k in range(CHUNKS):
+                c_v[a, k] = parts[k]
+            return carry
+
+        return lax.fori_loop(0, per, some, carry)
+
+    lax.fori_loop(0, 2, leaf_part, 0)
+    pl.semaphore_wait(pltpu.get_barrier_semaphore(), jnp.where(x == z, 28, 42))
 
     for first, dst, send, recv in ((10, wy_v, wy_send, wy_recv), (8, wz_v, wz_send, wz_recv)):
         for d in (1, 3, 2):
             to = (z + d) % RING
             remote(weights.at[pl.ds(first, 2), RING * y + to], dst.at[z], send, recv, (y, x, to, core)).start()
         pltpu.make_async_copy(weights.at[pl.ds(first, 2), RING * y + z], dst.at[z], recv).start()
+    lax.fori_loop(2, CHUNKS, leaf_part, 0)
 
     def forward_weights():
         pltpu.make_async_copy(wy_v, wy_v, wy_recv).wait()
@@ -110,21 +129,6 @@
             to = (x + d) % RING
             remote(wy_v.at[to], wx_v.at[x], wx_send, wx_recv, (y, to, z, core)).start()
         pltpu.make_async_copy(wy_v.at[x], wx_v.at[x], wx_recv).start()
-
-    def leaf_part(p, carry):
-        load_leaf(p).wait()
-        load_data(p).wait()
-
-        def some(j, carry):
-            a = p * per + j
-            parts = [dot(leaf_v[a, k], data_v[a, k]).astype(BF16) for k in range(CHUNKS)]
-            for k in range(CHUNKS):
-                c_v[a, k] = parts[k]
-            return carry
-
-        return lax.fori_loop(0, per, some, carry)
-
-    lax.fori_loop(0, CHUNKS, leaf_part, 0)
 
     def mix_blocks(level, pairs):
         mixed = [
@@ -167,90 +171,106 @@
         ]
         for a in range(GROUPS):
             e_v[a, k] = mixed[a]
+
+    def send_z(k, half):
+        part = pl.ds(half * HALF, HALF)
+        there = pl.ds(pl.multiple_of(y * HALF, HALF), HALF)
         for d in (5, 7, 13, 15, 1, 3, 4, 12, 6, 9, 11, 14, 2, 8, 10):
             ty, tz = (y + d // RING) % RING, (z + d % RING) % RING
-            remote(e_v.at[RING * ty + tz, k], z_v.at[k, y, z], z_send.at[k], z_recv.at[k], (ty, x, tz, core)).start()
-        pltpu.make_async_copy(e_v.at[RING * y + z, k], z_v.at[k, y, z], z_recv.at[k]).start()
-
-    def two_levels(k, w, get, put):
+            remote(
+                e_v.at[RING * ty + tz, k, :, part], z_v.at[k, half, z, :, there],
+                z_send.at[k, half], z_recv.at[k, half], (ty, x, tz, core),
+            ).start()
+        mine = e_v.at[RING * y + z, k, :, part]
+        pltpu.make_async_copy(mine, z_v.at[k, half, z, :, there], z_recv.at[k, half]).start()
+
+    def two_levels(k, w, held):
         first = [pair_weight(w[b, 0, k], w[b + 1, 0, k]) for b in (0, 2)]
         second = [pair_weight(w[b, 1, k], w[b + 2, 1, k]) for b in (0, 1)]
-        results = []
-        for q in range(RING):
-            b0, b1 = mix(first[0], get(0, q), get(1, q))
-            b2, b3 = mix(first[1], get(2, q), get(3, q))
-            results.append((b0, b1, b2, b3))
-        for q, (b0, b1, b2, b3) in enumerate(results):
-            b0, b2 = mix(second[0], b0, b2)
-            b1, b3 = mix(second[1], b1, b3)
-            results[q] = (b0, b1, b2, b3)
-        for q in range(RING):
-            for b in range(RING):
-                put(b, q, results[q][b])
-
-    def levels_z(k):
-        pltpu.make_async_copy(z_v.at[k], z_v.at[k], z_recv.at[k]).wait()
-
-        def put(b, q, value):
-            z_v[k, q, b] = value
-
-        two_levels(k, wz_v, lambda b, q: z_v[k, q, b], put)
+        b0, b1 = mix(first[0], held[0], held[1])
+        b2, b3 = mix(first[1], held[2], held[3])
+        b0, b2 = mix(second[0], b0, b2)
+        b1, b3 = mix(second[1], b1, b3)
+        for b, value in enumerate((b0, b1, b2, b3)):
+            held[b] = value
+
+    def levels_z(k, half):
+        held = z_v.at[k, half]
+        pltpu.make_async_copy(held, held, z_recv.at[k, half]).wait()
+        two_levels(k, wz_v, held)
         for d in (1, 3, 2):
             to = (x + d) % RING
-            remote(z_v.at[k, :, to], x_v.at[k, x], x_send.at[k], x_recv.at[k], (y, to, z, core)).start()
-        pltpu.make_async_copy(z_v.at[k, :, x], x_v.at[k, x], x_recv.at[k]).start()
-
-    def levels_x(k):
-        pltpu.make_async_copy(x_v.at[k], x_v.at[k], x_recv.at[k]).wait()
-
-        def put(b, q, value):
-            x_v[k, b, q] = value
-
-        two_levels(k, wx_v, lambda b, q: x_v[k, b, q], put)
-        for part in range(RING):
-            rows = jnp.concatenate([x_v[k, :, q].reshape(RING * R2, COLS) for q in range(RING)], axis=1)
-            total = dot(rows, table_v[:, pl.ds(part * COLS, COLS)])
+            remote(held.at[to], x_v.at[k, half, x], x_send.at[k, half], x_recv.at[k, half], (y, to, z, core)).start()
+        pltpu.make_async_copy(held.at[x], x_v.at[k, half, x], x_recv.at[k, half]).start()
+
+    def levels_x(k, half):
+        held = x_v.at[k, half]
+        pltpu.make_async_copy(held, held, x_recv.at[k, half]).wait()
+        two_levels(k, wx_v, held)
+
+    def slowness(k):
+        mine = RING * y + z
+        rows = jnp.concatenate([x_v[k, half].reshape(RING * R2, RING * HALF) for half in range(2)], axis=1)
+        for dy in (1, 3, 2, 0):
+            part = (y + dy) % RING
+            total = dot(rows, table_v[:, pl.ds(pl.multiple_of(part * COLS, COLS), COLS)])
             s_v[k, :, part] = total.astype(BF16).reshape(RING, R2, COLS)
-        mine = RING * y + z
-        for d in (5, 7, 13, 15, 1, 3, 4, 12, 6, 9, 11, 14, 2, 8, 10, 0):
-            ty, tx = (y + d // RING) % RING, (x + d % RING) % RING
-
-            def send_back(ty=ty, tx=tx):
-                remote(s_v.at[k, tx, ty], out.at[mine, k], back_send.at[k], back_recv.at[k], (ty, tx, x, core)).start()
-
-            if d == 0:
-                pl.when(x != z)(send_back)
-
-                @pl.when(x == z)
-                def _():
-                    pltpu.make_async_copy(s_v.at[k, x, y], out.at[mine, k], back_recv.at[k]).start()
-            else:
-                send_back()
+            for d in (1, 3, 2, 0):
+                tx = (x + d) % RING
+
+                def send_back(tx=tx):
+                    remote(s_v.at[k, tx, part], out.at[mine, k], back_send.at[k], back_recv.at[k], (part, tx, x, core)).start()
+
+                if d == 0 and dy == 0:
+                    pl.when(x != z)(send_back)
+
+                    @pl.when(x == z)
+                    def _():
+                        pltpu.make_async_copy(s_v.at[k, x, part], out.at[mine, k], back_recv.at[k]).start()
+                else:
+                    send_back()
 
     def step(t, carry):
-        pl.when(t < CHUNKS)(lambda: level_6(t))
-        pl.when((t >= 1) & (t < CHUNKS + 1))(lambda: level_7(t - 1))
+        now, before, last = t < CHUNKS, (t >= 2) & (t < CHUNKS + 2), t >= 3
+
+        pl.when(now)(lambda: level_6(t))
+
+        @pl.when((t >= 1) & (t < CHUNKS + 1))
+        def _():
+            level_7(t - 1)
+            send_z(t - 1, 0)
 
         @pl.when(t == 2)
         def _():
             pltpu.make_async_copy(wz_v, wz_v, wz_recv).wait()
 
-        pl.when((t >= 2) & (t < CHUNKS + 2))(lambda: levels_z(t - 2))
-
-        @pl.when(t == 3)
+        pl.when(before)(lambda: levels_z(t - 2, 0))
+        pl.when((t >= 1) & (t < CHUNKS + 1))(lambda: send_z(t - 1, 1))
+
+        @pl.when(last)
+        def _():
+            levels_x(t - 3, 1)
+            slowness(t - 3)
+
+        pl.when(before)(lambda: levels_z(t - 2, 1))
+
+        @pl.when(t == 2)
         def _():
             pltpu.make_async_copy(wx_v, wx_v, wx_recv).wait()
-            load_table.wait()
-
-        pl.when(t >= 3)(lambda: levels_x(t - 3))
+            pltpu.make_async_copy(table_v, table_v, table_sem).wait()
+
+        pl.when(before)(lambda: levels_x(t - 2, 0))
         return carry
 
     lax.fori_loop(0, CHUNKS + 3, step, 0)
 
     def finish(k, carry):
         send_core(k).wait_send()
-        pltpu.make_async_copy(e_v.at[pl.ds(0, 15), k], e_v.at[pl.ds(0, 15), k], z_send.at[k]).wait()
-        pltpu.make_async_copy(x_v.at[k, pl.ds(0, 3)], x_v.at[k, pl.ds(0, 3)], x_send.at[k]).wait()
+        for half in range(2):
+            sent = e_v.at[pl.ds(0, 15), k, :, pl.ds(half * HALF, HALF)]
+            pltpu.make_async_copy(sent, sent, z_send.at[k, half]).wait()
+            sent = x_v.at[k, half, pl.ds(0, 3)]
+            pltpu.make_async_copy(sent, sent, x_send.at[k, half]).wait()
 
         @pl.when(x != z)
         def _():
@@ -298,16 +318,16 @@
             vmem((GROUPS, CHUNKS, R2, COLS), BF16),
             vmem((GROUPS, CHUNKS, R2, COLS), BF16),
             vmem((GROUPS, CHUNKS, R2, COLS), BF16),
-            vmem((CHUNKS, RING, RING, R2, COLS), BF16),
-            vmem((CHUNKS, RING, RING, R2, COLS), BF16),
+            vmem((CHUNKS, 2, RING, R2, RING * HALF), BF16),
+            vmem((CHUNKS, 2, RING, R2, RING * HALF), BF16),
             vmem((CHUNKS, RING, RING, R2, COLS), BF16),
             vmem((RING, 2, CHUNKS, R2, TB), BF16),
             vmem((RING, 2, CHUNKS, R2, TB), BF16),
             vmem((RING, 2, CHUNKS, R2, TB), BF16),
             dma((CHUNKS,)), dma((CHUNKS,)), dma((8,)), dma,
             dma, dma, dma, dma, dma, dma,
-            dma((CHUNKS,)), dma((CHUNKS,)), dma((CHUNKS,)), dma((CHUNKS,)),
-            dma((CHUNKS,)), dma((CHUNKS,)), dma((CHUNKS,)), dma((CHUNKS,)),
+            dma((CHUNKS,)), dma((CHUNKS,)), dma((CHUNKS, 2)), dma((CHUNKS, 2)),
+            dma((CHUNKS, 2)), dma((CHUNKS, 2)), dma((CHUNKS,)), dma((CHUNKS,)),
         ],
         compiler_params=pltpu.CompilerParams(collective_id=0, has_side_effects=True, vmem_limit_bytes=58 << 20),
     )(
@@ -317,7 +337,7 @@
         slowness_table,
     )
     blocks = GROUPS * CHUNKS
-    step = 16
+    step = 32
     model = pl.pallas_call(
         model_kernel,
         grid=(blocks // step,),

time: 162 us -> 147 us (0.907)
  Pallas kernels: 162 us -> 146 us
    pallas_call x1, Pallas kernels: 152 us -> 138 us  [local(): pl.pallas_call(main_kernel, out_shape=jax.ShapeDtypeStruct((GROUPS, CHUNK...]
    pallas_call x1, Pallas kernels: 10.1 us -> 8.13 us  [local(): pl.pallas_call(model_kernel, grid=(blocks // step,), out_shape=jax.ShapeD...]
where the time goes in v3:
time: 147 us; the launch traced here: 146 us
  Pallas kernels  146 us (99%)
    pallas_call x1, Pallas kernels, local(): pl.pallas_call(main_kernel, out_shape=jax.ShapeDtypeStruct((GROUPS, CHUNK...  138 us
    pallas_call x1, Pallas kernels, local(): pl.pallas_call(model_kernel, grid=(blocks // step,), out_shape=jax.ShapeD...  8.13 us

profile of v3, /device:TPU:20, one launch (start us, length us, event | category | flops | bytes accessed | tf_op | source)
XLA Modules:
  0.0 145.7 jit_solution(2196505215798476486)
XLA Ops:
  0.0 137.6 %shard_map.55 = bf16[16,8,64,256]{3,2,1,0:T(8,128)(2,1)} custom-call(bf16[16,8,128,256]{3,2,1,0:T(8,128)(2,1)} %bitcast.7, bf16[16,8,64,128]{3,2,1,0:T(8,128)(2,1)} %bitcast.8, bf16[12,16,8,64,128]{4,3,2,1,0:T(8,128)(2,1)} %bitcast.5, bf16[1024,1024]{1,0:T(8,128)(2,1)} %table.1), custom_call_target="tpu_custom_call" | custom-call | tf_op jit(solution)/shard_map/pallas_call | solution.py:308
  137.6 8.1 %shard_map.56 = bf16[128,128,256]{2,1,0:T(8,128)(2,1)} custom-call(bf16[128,64,128]{2,1,0:T(8,128)(2,1)} %basis.1, bf16[128,64,256]{2,1,0:T(8,128)(2,1)} %bitcast.6), custom_call_target="tpu_custom_call" | custom-call | tf_op jit(solution)/shard_map/pallas_call | solution.py:341

commit v4 on v3

--- a/solution.py
+++ b/solution.py
@@ -13,6 +13,7 @@
 RING = 4
 GROUPS = RING * RING
 BATCH = 16
+PIECE = 32
 R2, TB, COLS = 64, 128, 256
 HALF = COLS // 2
 
@@ -288,17 +289,44 @@
         pltpu.make_async_copy(held.at[pl.ds(0, 3)], held.at[pl.ds(0, 3)], sem).wait()
 
 
-def model_kernel(basis, slow, out):
-    def some(j, carry):
+def model_kernel(basis, slow, out, basis_v, slow_v, out_v, basis_sem, slow_sem, out_sem):
+    def piece(ref, p):
+        return ref.at[pl.ds(p * PIECE, PIECE)]
+
+    def load(p):
+        return (
+            pltpu.make_async_copy(piece(basis, p), piece(basis_v, p), basis_sem.at[p]),
+            pltpu.make_async_copy(piece(slow, p), piece(slow_v, p), slow_sem.at[p]),
+        )
+
+    def store(p):
+        return pltpu.make_async_copy(piece(out_v, p), piece(out, p), out_sem.at[p])
+
+    pieces = basis.shape[0] // PIECE
+    for p in range(pieces):
+        for copy in load(p):
+            copy.start()
+
+    def some(p, carry):
+        for copy in load(p):
+            copy.wait()
+        at = [p * PIECE + u for u in range(PIECE)]
         rows = [
-            lax.dot_general(basis[n], slow[n], (((0,), (0,)), ((), ())), preferred_element_type=F32).astype(BF16)
-            for n in [j * BATCH + u for u in range(BATCH)]
+            lax.dot_general(basis_v[n], slow_v[n], (((0,), (0,)), ((), ())), preferred_element_type=F32).astype(BF16)
+            for n in at
         ]
-        for u in range(BATCH):
-            out[j * BATCH + u] = rows[u]
+        for u in range(PIECE):
+            out_v[at[u]] = rows[u]
+        store(p).start()
         return carry
 
-    lax.fori_loop(0, basis.shape[0] // BATCH, some, 0)
+    lax.fori_loop(0, pieces, some, 0)
+
+    def finish(p, carry):
+        store(p).wait()
+        return carry
+
+    lax.fori_loop(0, pieces, finish, 0)
 
 
 def local(data, leaf_basis, level_weights, slowness_table, model_basis):
@@ -337,16 +365,16 @@
         slowness_table,
     )
     blocks = GROUPS * CHUNKS
-    step = 32
+    pieces = blocks // PIECE
     model = pl.pallas_call(
         model_kernel,
-        grid=(blocks // step,),
         out_shape=jax.ShapeDtypeStruct((blocks, TB, COLS), BF16),
-        in_specs=[
-            pl.BlockSpec((step, R2, TB), lambda n: (n, 0, 0)),
-            pl.BlockSpec((step, R2, COLS), lambda n: (n, 0, 0)),
+        in_specs=[any_space] * 2,
+        out_specs=any_space,
+        scratch_shapes=[
+            vmem((blocks, R2, TB), BF16), vmem((blocks, R2, COLS), BF16), vmem((blocks, TB, COLS), BF16),
+            dma((pieces,)), dma((pieces,)), dma((pieces,)),
         ],
-        out_specs=pl.BlockSpec((step, TB, COLS), lambda n: (n, 0, 0)),
         compiler_params=pltpu.CompilerParams(vmem_limit_bytes=58 << 20),
     )(model_basis, slow.reshape(blocks, R2, COLS))
     return model.reshape(blocks * TB, COLS)

time: 147 us -> 145 us (0.986)
  Pallas kernels: 146 us -> 143 us
    pallas_call x1, Pallas kernels: 8.13 us -> 5.8 us  [local(): pl.pallas_call(model_kernel, out_shape=jax.ShapeDtypeStruct((blocks, TB,...]
where the time goes in v4:
time: 145 us; the launch traced here: 143 us
  Pallas kernels  143 us (99%)
    pallas_call x1, Pallas kernels, local(): pl.pallas_call(main_kernel, out_shape=jax.ShapeDtypeStruct((GROUPS, CHUNK...  138 us
    pallas_call x1, Pallas kernels, local(): pl.pallas_call(model_kernel, out_shape=jax.ShapeDtypeStruct((blocks, TB,...  5.8 us

profile of v4, /device:TPU:20, one launch (start us, length us, event | category | flops | bytes accessed | tf_op | source)
XLA Modules:
  0.0 143.4 jit_solution(12114036572937530052)
XLA Ops:
  0.0 137.6 %shard_map.55 = bf16[16,8,64,256]{3,2,1,0:T(8,128)(2,1)} custom-call(bf16[16,8,128,256]{3,2,1,0:T(8,128)(2,1)} %bitcast.7, bf16[16,8,64,128]{3,2,1,0:T(8,128)(2,1)} %bitcast.8, bf16[12,16,8,64,128]{4,3,2,1,0:T(8,128)(2,1)} %bitcast.5, bf16[1024,1024]{1,0:T(8,128)(2,1)} %table.1), custom_call_target="tpu_custom_call" | custom-call | tf_op jit(solution)/shard_map/pallas_call | solution.py:336
  137.6 5.8 %shard_map.56 = bf16[128,128,256]{2,1,0:T(8,128)(2,1)} custom-call(bf16[128,64,128]{2,1,0:T(8,128)(2,1)} %basis.1, bf16[128,64,256]{2,1,0:T(8,128)(2,1)} %bitcast.6), custom_call_target="tpu_custom_call" | custom-call | tf_op jit(solution)/shard_map/pallas_call | solution.py:369

commit v5 on v4

--- a/solution.py
+++ b/solution.py
@@ -73,6 +73,7 @@
     core_send, core_recv, z_send, z_recv, x_send, x_recv, back_send, back_recv,
 ):
     y, x, z, core = place()
+    turn = 1 + 2 * core
     per = GROUPS // CHUNKS
 
     def load_data(p):
@@ -213,11 +214,11 @@
         mine = RING * y + z
         rows = jnp.concatenate([x_v[k, half].reshape(RING * R2, RING * HALF) for half in range(2)], axis=1)
         for dy in (1, 3, 2, 0):
-            part = (y + dy) % RING
+            part = (y + dy * turn) % RING
             total = dot(rows, table_v[:, pl.ds(pl.multiple_of(part * COLS, COLS), COLS)])
             s_v[k, :, part] = total.astype(BF16).reshape(RING, R2, COLS)
             for d in (1, 3, 2, 0):
-                tx = (x + d) % RING
+                tx = (x + d * turn) % RING
 
                 def send_back(tx=tx):
                     remote(s_v.at[k, tx, part], out.at[mine, k], back_send.at[k], back_recv.at[k], (part, tx, x, core)).start()

time: 145 us -> 144 us (level)
  no operation moved by 1% of the time
where the time goes in v5:
time: 144 us; the launch traced here: 143 us
  Pallas kernels  143 us (99%)
    pallas_call x1, Pallas kernels, local(): pl.pallas_call(main_kernel, out_shape=jax.ShapeDtypeStruct((GROUPS, CHUNK...  137 us
    pallas_call x1, Pallas kernels, local(): pl.pallas_call(model_kernel, out_shape=jax.ShapeDtypeStruct((blocks, TB,...  5.81 us

profile of v5, /device:TPU:20, one launch (start us, length us, event | category | flops | bytes accessed | tf_op | source)
XLA Modules:
  0.0 143.0 jit_solution(4603647750444357286)
XLA Ops:
  0.0 137.2 %shard_map.55 = bf16[16,8,64,256]{3,2,1,0:T(8,128)(2,1)} custom-call(bf16[16,8,128,256]{3,2,1,0:T(8,128)(2,1)} %bitcast.7, bf16[16,8,64,128]{3,2,1,0:T(8,128)(2,1)} %bitcast.8, bf16[12,16,8,64,128]{4,3,2,1,0:T(8,128)(2,1)} %bitcast.5, bf16[1024,1024]{1,0:T(8,128)(2,1)} %table.1), custom_call_target="tpu_custom_call" | custom-call | tf_op jit(solution)/shard_map/pallas_call | solution.py:337
  137.2 5.8 %shard_map.56 = bf16[128,128,256]{2,1,0:T(8,128)(2,1)} custom-call(bf16[128,64,128]{2,1,0:T(8,128)(2,1)} %basis.1, bf16[128,64,256]{2,1,0:T(8,128)(2,1)} %bitcast.6), custom_call_target="tpu_custom_call" | custom-call | tf_op jit(solution)/shard_map/pallas_call | solution.py:370
